TPU v7x, 256 devices: a whole 4x4x8 slice. The times are simulated.
256 devices in a mesh: dp: 64 (over x, y_hi, z), ctx: 4 (over y_lo, core).
Axes of the slice: x: 4, y: 4 (y_hi: 2, y_lo: 2; y = y_hi * 2 + y_lo), z: 8, core: 2. Of those that a mesh axis runs over, the one named last changes fastest.
Arguments:
- frames: bfloat16 [64, 1024, 1536], P('dp', 'ctx'), may hold values from -6 to 6
- destinations: int32 [64, 1024], P('dp', 'ctx'), may hold values from 0 to 16383, as said below
- segments: int32 [64, 1024], P('dp'), may hold values from 0 to 2, as said below
- tile_mask: int32 [64, 8, 8], P('dp', 'ctx'), may hold values from 0 to 1, as said below
- attn_gain: float32 [1536], replicated, may hold values from 0.1 to 1.9
- w_qkv: bfloat16 [1536, 2304], replicated
- w_out: bfloat16 [768, 1536], replicated, may hold values from -5 to 5
- conv_gain: float32 [1536], replicated, may hold values from 0.1 to 1.9
- w_pointin: bfloat16 [1536, 1536], P(('dp', 'ctx')), may hold values from -0.625 to 0.625
- w_pointout: bfloat16 [768, 1536], P(None, ('dp', 'ctx')), may hold values from -0.43164062 to 0.43164062
- w_depth: float32 [32, 768], replicated, may hold values from -1 to 1
- bn_scale: float32 [768], replicated, may hold values from 0.1 to 1.9
- bn_shift: float32 [768], replicated, may hold values from -3 to 3
Outputs:
- layer_out: bfloat16 [64, 1024, 1536], P('dp', 'ctx')
Inputs may be any that keep to these rules, and one draw needn't show every extreme that they name: `destinations`: per ctx index c, the values at positions c * 256 to (c + 1) * 256 - 1 over all rows of the first dimension are all different, so every target row is filled once. The rows of one device send at most 8 frames to one sequence, and exactly 8 to some sequences. `segments`: along a sequence the ids never fall, start at 0 and end at 2. tile_mask[b, t, t] = 1; tile_mask[b, t, u] = 0 where tiles t and u of sequence b share no segment id.
All inputs are finite; a program needn't handle non-finite values.
Results may differ from a plain program's by a relative error of at most 0.01.
Values may be sent and summed in bfloat16 or wider, within the bound.
A program may use at most 128 MiB of HBM per device.

v0:
```python
import math
import jax
import jax.numpy as jnp
from jax import lax
from jax.sharding import PartitionSpec as P

HEADS = 8


def padded_2(cells, sides, width):
    for axis, dim in sides:
        count = lax.axis_size(axis)
        ends = count - 1
        head = lax.slice_in_dim(cells, 0, width, axis=dim)
        tail = lax.slice_in_dim(cells, cells.shape[dim] - width, cells.shape[dim], axis=dim)
        cells = jnp.concatenate(
            [
                lax.ppermute(tail, axis, [(i, (i + 1) % count) for i in range(ends)]),
                cells,
                lax.ppermute(head, axis, [((i + 1) % count, i) for i in range(ends)]),
            ],
            axis=dim,
        )
    return cells


def layer_norm(values, gain):
    as_float = values.astype(jnp.float32)
    row_mean = jnp.mean(as_float, axis=-1, keepdims=True)
    centred = as_float - row_mean
    row_var = jnp.mean(centred * centred, axis=-1, keepdims=True)
    return centred * lax.rsqrt(row_var + 1e-06) * gain


def per_device(
    frames,
    destinations,
    segments,
    tile_mask,
    attn_gain,
    w_qkv,
    w_out,
    conv_gain,
    w_pointin,
    w_pointout,
    w_depth,
    bn_scale,
    bn_shift,
):
    row_count = frames.shape[1]
    width = frames.shape[2]
    peer_count = lax.axis_size("dp")
    capacity = 2 * row_count // peer_count
    own_frames = frames[0]
    targets = destinations[0]
    owner_index = targets // row_count
    slot_index = targets % row_count
    onehot = (owner_index[:, None] == jnp.arange(peer_count, dtype=jnp.int32)[None, :]).astype(
        jnp.int32
    )
    before = jnp.cumsum(onehot, axis=0) - onehot
    rank_in = jnp.sum(before * onehot, axis=1)
    position = owner_index * capacity + rank_in
    send_rows = jnp.zeros((peer_count * capacity, width), jnp.bfloat16).at[position].set(own_frames)
    send_slots = (
        jnp.full((peer_count * capacity,), row_count, jnp.int32).at[position].set(slot_index)
    )
    got_rows, got_slots = (
        lax.all_to_all(
            send_rows.reshape(peer_count, capacity, width),
            "dp",
            split_axis=0,
            concat_axis=0,
            tiled=True,
        ),
        lax.all_to_all(
            send_slots.reshape(peer_count, capacity), "dp", split_axis=0, concat_axis=0, tiled=True
        ),
    )
    placed = (
        jnp.zeros((row_count, width), jnp.bfloat16)
        .at[got_slots.reshape(-1)]
        .set(got_rows.reshape(-1, width), mode="drop")
    )
    shard_start = lax.axis_index("ctx") * row_count
    seg_row = segments[0]
    own_seg = lax.dynamic_slice_in_dim(seg_row, shard_start, row_count, 0)
    mask_rows = tile_mask[0]
    tile_size = row_count // mask_rows.shape[0]
    head_cols = w_out.shape[0]
    head_size = head_cols // HEADS
    scale_factor = 1.0 / math.sqrt(head_size)
    normed = layer_norm(placed, attn_gain).astype(jnp.bfloat16)
    qkv_rows = jnp.dot(normed, w_qkv, preferred_element_type=jnp.float32).astype(jnp.bfloat16)
    queries = qkv_rows[:, :head_cols].reshape(row_count, HEADS, head_size)
    key_rows = qkv_rows[:, head_cols : 2 * head_cols].reshape(row_count, HEADS, head_size)
    value_rows = qkv_rows[:, 2 * head_cols :].reshape(row_count, HEADS, head_size)

    def absorb(carry, block):
        key_block, value_block, seg_block, mask_block = block
        wide_mask = jnp.repeat(jnp.repeat(mask_block, tile_size, axis=0), tile_size, axis=1)
        allowed = (own_seg[:, None] == seg_block[None, :]) & (wide_mask == 1)
        running_max, running_sum, weighted = carry
        scores = (
            jnp.einsum("qhd,khd->hqk", queries, key_block, preferred_element_type=jnp.float32)
            * scale_factor
        )
        scores = jnp.where(allowed[None], scores, -1e30)
        new_max = jnp.maximum(running_max, jnp.max(scores, axis=-1))
        weights = jnp.where(allowed[None], jnp.exp(scores - new_max[:, :, None]), 0.0)
        factor = jnp.exp(running_max - new_max)
        new_sum = running_sum * factor + jnp.sum(weights, axis=-1)
        product = jnp.einsum(
            "hqk,khd->hqd",
            weights.astype(jnp.bfloat16),
            value_block,
            preferred_element_type=jnp.float32,
        )
        return ((new_max, new_sum, weighted * factor[:, :, None] + product), None)

    start_state = (
        jnp.full((HEADS, row_count), -1e30, jnp.float32),
        jnp.zeros((HEADS, row_count), jnp.float32),
        jnp.zeros((HEADS, row_count, head_size), jnp.float32),
    )
    keys_piece = lax.all_gather(key_rows, "ctx", axis=0, tiled=True)
    values_piece = lax.all_gather(value_rows, "ctx", axis=0, tiled=True)
    count = keys_piece.shape[0]
    block_rows = math.gcd(count, 512)
    blocks = count // block_rows
    mask_piece = mask_rows
    mask_piece = jnp.transpose(
        mask_piece.reshape(mask_rows.shape[0], blocks, block_rows // tile_size), (1, 0, 2)
    )
    inputs = (
        keys_piece.reshape(blocks, block_rows, HEADS, head_size),
        values_piece.reshape(blocks, block_rows, HEADS, head_size),
        seg_row.reshape(blocks, block_rows),
        mask_piece,
    )
    result, unused = lax.scan(absorb, start_state, inputs)
    final_max, final_sum, weighted = result
    attended = (
        jnp.transpose(weighted / final_sum[:, :, None], (1, 0, 2))
        .reshape(row_count, head_cols)
        .astype(jnp.bfloat16)
    )
    branch = jnp.dot(attended, w_out, preferred_element_type=jnp.float32)
    after_attn = (placed.astype(jnp.float32) + branch).astype(jnp.bfloat16)
    conv_normed = layer_norm(after_attn, conv_gain).astype(jnp.bfloat16)
    channels = w_depth.shape[1]
    projected = jnp.dot(
        conv_normed,
        lax.all_gather(w_pointin, ("dp", "ctx"), axis=0, tiled=True),
        preferred_element_type=jnp.float32,
    )
    gated = (projected[:, :channels] * jax.nn.sigmoid(projected[:, channels:])).astype(jnp.bfloat16)
    kernel_len = w_depth.shape[0]
    half_len = kernel_len // 2
    padded = padded_2(gated, (("ctx", 0),), half_len)
    padded_f = padded.astype(jnp.float32)
    seg_pad = jnp.pad(seg_row, (half_len, half_len), constant_values=-1)
    seg_near = lax.dynamic_slice_in_dim(seg_pad, shard_start, row_count + 2 * half_len, 0)
    depthwise = jnp.zeros((row_count, channels), jnp.float32)
    for tap_index in range(kernel_len):
        same_seg = (seg_near[tap_index : tap_index + row_count] == own_seg).astype(jnp.float32)
        depthwise = (
            depthwise
            + w_depth[tap_index][None, :]
            * padded_f[tap_index : tap_index + row_count]
            * same_seg[:, None]
        )
    shifted = depthwise * bn_scale + bn_shift
    activated = (shifted * jax.nn.sigmoid(shifted)).astype(jnp.bfloat16)
    closing = jnp.dot(
        activated,
        lax.all_gather(w_pointout, ("dp", "ctx"), axis=1, tiled=True),
        preferred_element_type=jnp.float32,
    )
    layer_out = (after_attn.astype(jnp.float32) + closing).astype(jnp.bfloat16)
    return layer_out[None]


def solution(mesh):
    return jax.shard_map(
        per_device,
        mesh=mesh,
        in_specs=(
            P("dp", "ctx", None),
            P("dp", "ctx"),
            P("dp", None),
            P("dp", "ctx", None),
            P(),
            P(),
            P(),
            P(),
            P(("dp", "ctx"), None),
            P(None, ("dp", "ctx")),
            P(),
            P(),
            P(),
        ),
        out_specs=P("dp", "ctx", None),
        check_vma=False,
    )
```

profile of v0, /device:TPU:32, one launch (start us, length us, event | category | flops | bytes accessed | tf_op | source)
XLA Modules:
  0.0 1003.4 jit_solution(10388988709967639840)
XLA Ops:
  9.7 1.4 scatter_custom_fusion
  11.8 14.2 %all-to-all-start = ((s32[64,1,8]{2,1,0:T(1,128)}), s32[64,1,8]{2,1,0:T(1,128)S(1)}, u32[]{:S(2)}, u32[]{:S(2)}) async-start(s32[64,1,8]{2,1,0:T(1,128)} %bitcast.6), calls=%async_computation | async-start | bytes 65536 | tf_op jit(solution)/shard_map/all_to_all | solution.py:76
  26.1 3.7 scatter_custom_fusion.1
  29.8 7.1 all-to-all-done
  36.9 6.3 all-to-all-start.1
  44.7 39.0 %all-to-all-done.1 = bf16[64,8,1536]{2,1,0:T(8,128)(2,1)} async-done(((bf16[64,8,1536]{2,1,0:T(8,128)(2,1)}), bf16[64,8,1536]{2,1,0:T(8,128)(2,1)}, u32[]{:S(2)}, u32[]{:S(2)}) %all-to-all-start.1) | async-done | bytes 1572896 | tf_op jit(solution)/shard_map/all_to_all | solution.py:69
  83.7 4.0 scatter_custom_fusion.2
  88.3 5.1 convolution_convert_fusion
  93.4 0.9 fusion.120
  94.4 2.0 copy.31
  96.4 1.9 copy.29
  102.3 15.2 %all-gather.9.cloned.1.call-done = bf16[1024,8,96]{0,2,1:T(8,128)(2,1)} async-done(((bf16[256,8,96]{0,2,1:T(8,128)(2,1)}), bf16[1024,8,96]{0,2,1:T(8,128)(2,1)}) %all-gather.9.cloned.1.call-update) | async-done | bytes 1572880 | tf_op jit(solution)/shard_map/all_gather | solution.py:127
  117.5 2.7 copy.43
  120.2 27.3 %all-gather.7.cloned.1.call-done = bf16[1024,8,96]{0,2,1:T(8,128)(2,1)} async-done(((bf16[256,8,96]{0,2,1:T(8,128)(2,1)}), bf16[1024,8,96]{0,2,1:T(8,128)(2,1)}) %all-gather.7.cloned.1.call-update) | async-done | bytes 1572880 | tf_op jit(solution)/shard_map/all_gather | solution.py:126
  147.5 2.7 copy.44
  150.3 22.4 %while.15 = (s32[]{:T(128)}, f32[8,256]{1,0:T(8,128)S(1)}, f32[8,256]{1,0:T(8,128)S(1)}, f32[8,256,96]{1,2,0:T(8,128)}, s32[256]{0:T(256)S(1)}, /*index=5*/s32[2...) while((s32[]{:T(128)}, f32[8,256]{1,0:T(8,128)S(1)}, ...), condition=%wide.region_11.12_spmd.clone, body=%wide.region_8.11_spmd.clone.sunk | while | flops 417146880 | bytes 33564948 | solution.py:141
  150.6 4.1 fusion.139
  154.6 3.3 fusion.140
  158.1 3.3 fusion.142
  161.6 4.1 fusion.139
  165.7 3.4 fusion.140
  169.1 3.5 fusion.142
  172.7 1.3 divide_convert_fusion
  174.9 1.1 copy-done.4
  176.4 394.0 %all-gather.11.cloned.1.call-done = bf16[256,6,1536]{2,1,0:T(8,128)(2,1)} async-done(((bf16[1,6,1536]{2,1,0:T(8,128)(2,1)}), bf16[256,6,1536]{2,1,0:T(8,128)(2,1)}) %all-gather.11.cloned.1.call-update) | async-done | bytes 4718608 | tf_op jit(solution)/shard_map/all_gather | solution.py:154
  570.4 8.5 reshape.317
  578.8 4.3 fusion.31
  583.3 1.3 collective-permute-start
  584.6 1.3 collective-permute-start.1
  586.3 396.1 %all-gather.13.cloned.1.call-done = bf16[256,6,768]{2,1,0:T(8,128)(2,1)} async-done(((bf16[1,6,768]{2,1,0:T(8,128)(2,1)}), bf16[256,6,768]{2,1,0:T(8,128)(2,1)}) %all-gather.13.cloned.1.call-update) | async-done | bytes 2359312 | tf_op jit(solution)/shard_map/all_gather | solution.py:177
  982.3 5.1 reshape.319
  987.7 9.2 fusion.23
  (123 shorter events, 12.4 us)
Async XLA Ops:
  6.5 167.4 %copy-start = (bf16[768,1536]{1,0:T(8,128)(2,1)S(1)}, bf16[768,1536]{1,0:T(8,128)(2,1)}, u32[]{:S(2)}) copy-start(bf16[768,1536]{1,0:T(8,128)(2,1)} %param.21) | copy-start | bytes 7077892
  11.8 25.1 %all-to-all-start = ((s32[64,1,8]{2,1,0:T(1,128)}), s32[64,1,8]{2,1,0:T(1,128)S(1)}, u32[]{:S(2)}, u32[]{:S(2)}) async-start(s32[64,1,8]{2,1,0:T(1,128)} %bitcast.6), calls=%async_computation | async-start | bytes 65536 | tf_op jit(solution)/shard_map/all_to_all | solution.py:76
  36.9 46.8 %all-to-all-start.1 = ((bf16[64,8,1536]{2,1,0:T(8,128)(2,1)}), bf16[64,8,1536]{2,1,0:T(8,128)(2,1)}, u32[]{:S(2)}, u32[]{:S(2)}) async-start(bf16[64,8,1536]{2,1,0:T(8,128)(2,1)} %bitcast.124), calls=%async_computation.1 | async-start | bytes 3145728 | tf_op jit(solution)/shard_map/all_to_all | solution.py:69
  43.2 74.3 %all-gather.9.cloned.1.call-start = ((), (), s32[]{:S(2)}) async-start(), calls=%async_computation.3 | async-start | bytes 1966080 | tf_op jit(solution)/shard_map/all_gather | solution.py:127
  87.7 5.7 copy-start.2
  94.4 7.5 copy-start.7
  94.4 7.6 copy-start.5
  96.4 51.2 %all-gather.7.cloned.1.call-start = ((), (), s32[]{:S(2)}) async-start(), calls=%async_computation.2 | async-start | bytes 1966080 | tf_op jit(solution)/shard_map/all_gather | solution.py:126
  98.4 472.0 %all-gather.11.cloned.1.call-start = ((), (), s32[]{:S(2)}) async-start(), calls=%async_computation.4 | async-start | bytes 6316032 | tf_op jit(solution)/shard_map/all_gather | solution.py:154
  99.1 883.2 %all-gather.13.cloned.1.call-start = ((), (), s32[]{:S(2)}) async-start(), calls=%async_computation.5 | async-start | bytes 3158016 | tf_op jit(solution)/shard_map/all_gather | solution.py:177
  176.4 402.5 %copy-start.26 = (f32[1536]{0:T(1024)S(1)}, f32[1536]{0:T(1024)}, u32[]{:S(2)}) copy-start(f32[1536]{0:T(1024)} %param.22) | copy-start | bytes 18436
  583.3 404.1 %collective-permute-start = (bf16[16,768]{1,0:T(8,128)(2,1)S(1)}, bf16[16,768]{1,0:T(8,128)(2,1)S(1)}, u32[]{:S(2)}, u32[]{:S(2)}) collective-permute-start(bf16[16,768]{1,0:T(8,128)(2,1)S(1)} %get-tuple-element.182), channel_id=1, source_target_pairs={{0,1},{1,2},{2,3},{4,5},{5,6},{6,7},{8,9},{9,10},{10,11},{12,13},{... | collective-permute-start | bytes 73736 | tf_op jit(solution)/shard_map/ppermute | solution.py:18
  584.6 402.8 %collective-permute-start.1 = (bf16[16,768]{1,0:T(8,128)(2,1)S(1)}, bf16[16,768]{1,0:T(8,128)(2,1)S(1)}, u32[]{:S(2)}, u32[]{:S(2)}) collective-permute-start(bf16[16,768]{1,0:T(8,128)(2,1)S(1)} %get-tuple-element.183), channel_id=1, source_target_pairs={{1,0},{2,1},{3,2},{5,4},{6,5},{7,6},{9,8},{10,9},{11,10},{13,12},{... | collective-permute-start | bytes 73736 | tf_op jit(solution)/shard_map/ppermute | solution.py:20
  586.1 401.4 %copy-start.8 = (f32[256]{0:T(256)S(1)}, f32[256]{0:T(256)}, u32[]{:S(2)}) copy-start(f32[256]{0:T(256)} %get-tuple-element.199) | copy-start | bytes 3076
  586.1 401.4 %copy-start.9 = (f32[256]{0:T(256)S(1)}, f32[256]{0:T(256)}, u32[]{:S(2)}) copy-start(f32[256]{0:T(256)} %get-tuple-element.200) | copy-start | bytes 3076
  586.1 401.4 %copy-start.10 = (f32[256]{0:T(256)S(1)}, f32[256]{0:T(256)}, u32[]{:S(2)}) copy-start(f32[256]{0:T(256)} %get-tuple-element.201) | copy-start | bytes 3076
  586.1 401.4 %copy-start.11 = (f32[256]{0:T(256)S(1)}, f32[256]{0:T(256)}, u32[]{:S(2)}) copy-start(f32[256]{0:T(256)} %get-tuple-element.202) | copy-start | bytes 3076
  586.1 401.4 %copy-start.12 = (f32[256]{0:T(256)S(1)}, f32[256]{0:T(256)}, u32[]{:S(2)}) copy-start(f32[256]{0:T(256)} %get-tuple-element.203) | copy-start | bytes 3076
  586.1 401.4 %copy-start.13 = (f32[256]{0:T(256)S(1)}, f32[256]{0:T(256)}, u32[]{:S(2)}) copy-start(f32[256]{0:T(256)} %get-tuple-element.204) | copy-start | bytes 3076
  586.1 401.4 %copy-start.14 = (f32[256]{0:T(256)S(1)}, f32[256]{0:T(256)}, u32[]{:S(2)}) copy-start(f32[256]{0:T(256)} %get-tuple-element.205) | copy-start | bytes 3076
  586.1 401.4 %copy-start.15 = (f32[256]{0:T(256)S(1)}, f32[256]{0:T(256)}, u32[]{:S(2)}) copy-start(f32[256]{0:T(256)} %get-tuple-element.206) | copy-start | bytes 3076
  586.1 401.4 %copy-start.16 = (f32[256]{0:T(256)S(1)}, f32[256]{0:T(256)}, u32[]{:S(2)}) copy-start(f32[256]{0:T(256)} %get-tuple-element.207) | copy-start | bytes 3076
  586.1 401.4 %copy-start.17 = (f32[256]{0:T(256)S(1)}, f32[256]{0:T(256)}, u32[]{:S(2)}) copy-start(f32[256]{0:T(256)} %get-tuple-element.208) | copy-start | bytes 3076
  586.2 401.4 %copy-start.18 = (f32[256]{0:T(256)S(1)}, f32[256]{0:T(256)}, u32[]{:S(2)}) copy-start(f32[256]{0:T(256)} %get-tuple-element.209) | copy-start | bytes 3076
  586.2 401.4 %copy-start.19 = (f32[256]{0:T(256)S(1)}, f32[256]{0:T(256)}, u32[]{:S(2)}) copy-start(f32[256]{0:T(256)} %get-tuple-element.210) | copy-start | bytes 3076
  586.2 401.4 %copy-start.20 = (f32[256]{0:T(256)S(1)}, f32[256]{0:T(256)}, u32[]{:S(2)}) copy-start(f32[256]{0:T(256)} %get-tuple-element.211) | copy-start | bytes 3076
  586.2 401.4 %copy-start.21 = (f32[256]{0:T(256)S(1)}, f32[256]{0:T(256)}, u32[]{:S(2)}) copy-start(f32[256]{0:T(256)} %get-tuple-element.212) | copy-start | bytes 3076
  586.2 401.4 %copy-start.22 = (f32[256]{0:T(256)S(1)}, f32[256]{0:T(256)}, u32[]{:S(2)}) copy-start(f32[256]{0:T(256)} %get-tuple-element.213) | copy-start | bytes 3076
  586.2 401.4 %copy-start.23 = (f32[256]{0:T(256)S(1)}, f32[256]{0:T(256)}, u32[]{:S(2)}) copy-start(f32[256]{0:T(256)} %get-tuple-element.214) | copy-start | bytes 3076
  586.2 401.4 %copy-start.24 = (f32[256]{0:T(256)S(1)}, f32[256]{0:T(256)}, u32[]{:S(2)}) copy-start(f32[256]{0:T(256)} %get-tuple-element.215) | copy-start | bytes 3076
  586.2 401.4 %copy-start.27 = (f32[768]{0:T(1024)S(1)}, f32[768]{0:T(1024)}, u32[]{:S(2)}) copy-start(f32[768]{0:T(1024)} %param.27) | copy-start | bytes 9220
  586.2 401.4 %copy-start.28 = (f32[768]{0:T(1024)S(1)}, f32[768]{0:T(1024)}, u32[]{:S(2)}) copy-start(f32[768]{0:T(1024)} %param.26) | copy-start | bytes 9220
  (6 other events, 19.3 us)
Sparse Core Ops, SparseCore 0:
  96.5 20.9 all-gather.8
  119.3 28.2 all-gather.6
  149.4 420.8 all-gather.10
  572.1 410.1 all-gather.12
where the time goes:
time: 1000 us
  waiting for transfers between devices  880 us (88%)
  local copies, waits for them, and re-layouts  36.8 us (4%)
  matrix products  34.4 us (3%)
  starting transfers between devices  23.4 us (2%)
  other arithmetic  15.3 us (2%)
  between operations  13.7 us (1%)
    all_gather x1, waiting for transfers between devices, per_device(): lax.all_gather(w_pointout, ('dp', 'ctx'), axis=1, tiled=True)  396 us
    all_gather x1, waiting for transfers between devices, per_device(): lax.all_gather(w_pointin, ('dp', 'ctx'), axis=0, tiled=True)  394 us
    all_to_all x1, waiting for transfers between devices, per_device(): lax.all_to_all(send_rows.reshape(peer_count, capacity, width), 'dp', spli...  39 us
    all_gather x1, waiting for transfers between devices, per_device(): keys_piece = lax.all_gather(key_rows, 'ctx', axis=0, tiled=True)  27.3 us
  transfers between devices with their start and end apart: 8, of which 6 were waited for; matrix products, arithmetic and copies ran while one was open for 6% of the time, Pallas kernels for 0%

commit v1 on v0

--- a/solution.py
+++ b/solution.py
@@ -5,6 +5,11 @@
 from jax.sharding import PartitionSpec as P
 
 HEADS = 8
+
+
+def gather_over(x, mesh_axis, along):
+    sent = jnp.stack([x] * lax.axis_size(mesh_axis))
+    return jnp.concatenate(lax.all_to_all(sent, mesh_axis, 0, 0), axis=along)
 
 
 def padded_2(cells, sides, width):
@@ -150,9 +155,7 @@
     conv_normed = layer_norm(after_attn, conv_gain).astype(jnp.bfloat16)
     channels = w_depth.shape[1]
     projected = jnp.dot(
-        conv_normed,
-        lax.all_gather(w_pointin, ("dp", "ctx"), axis=0, tiled=True),
-        preferred_element_type=jnp.float32,
+        conv_normed, gather_over(w_pointin, ("dp", "ctx"), 0), preferred_element_type=jnp.float32
     )
     gated = (projected[:, :channels] * jax.nn.sigmoid(projected[:, channels:])).astype(jnp.bfloat16)
     kernel_len = w_depth.shape[0]

time: 1000 us -> 637 us (0.64); the launches traced: 1000 us -> 627 us
  waiting for transfers between devices: 880 us -> 493 us
    all_gather x1 -> x0, waiting for transfers between devices: 394 us -> none  [per_device(): lax.all_gather(w_pointin, ('dp', 'ctx'), axis=0, tiled=True)]
    all_gather x1, waiting for transfers between devices: 396 us -> 341 us  [per_device(): lax.all_gather(w_pointout, ('dp', 'ctx'), axis=1, tiled=True)]
    all_to_all x0 -> x1, waiting for transfers between devices: none -> 38.7 us  [gather_over(): return jnp.concatenate(lax.all_to_all(sent, mesh_axis, 0, 0), axis=along)]
    all_gather x1, waiting for transfers between devices: 27.3 us -> 40.2 us  [per_device(): keys_piece = lax.all_gather(key_rows, 'ctx', axis=0, tiled=True)]
    all_gather x1, waiting for transfers between devices: 15.2 us -> 26.4 us  [per_device(): values_piece = lax.all_gather(value_rows, 'ctx', axis=0, tiled=True)]
  transfers between devices with their start and end apart: 8 -> 8, of which waited for: 6 -> 6; matrix products, arithmetic and copies ran while one was open for 6% -> 10% of each run, Pallas kernels for 0% -> 0%
where the time goes in v1:
time: 637 us; the launch traced here: 627 us
  waiting for transfers between devices  493 us (77%)
  local copies, waits for them, and re-layouts  39.6 us (6%)
  matrix products  34.2 us (5%)
  starting transfers between devices  31.2 us (5%)
  other arithmetic  15 us (2%)
  between operations  13.7 us (2%)
    all_gather x1, waiting for transfers between devices, per_device(): lax.all_gather(w_pointout, ('dp', 'ctx'), axis=1, tiled=True)  341 us
    all_gather x1, waiting for transfers between devices, per_device(): keys_piece = lax.all_gather(key_rows, 'ctx', axis=0, tiled=True)  40.2 us
    all_to_all x1, waiting for transfers between devices, per_device(): lax.all_to_all(send_rows.reshape(peer_count, capacity, width), 'dp', spli...  39.3 us
    all_to_all x1, waiting for transfers between devices, gather_over(): return jnp.concatenate(lax.all_to_all(sent, mesh_axis, 0, 0), axis=along)  38.7 us
    all_gather x1, waiting for transfers between devices, per_device(): values_piece = lax.all_gather(value_rows, 'ctx', axis=0, tiled=True)  26.4 us
    all_to_all x1, starting transfers between devices, per_device(): lax.all_to_all(send_slots.reshape(peer_count, capacity), 'dp', split_axis...  14.2 us
  transfers between devices with their start and end apart: 8, of which 6 were waited for; matrix products, arithmetic and copies ran while one was open for 10% of the time, Pallas kernels for 0%

profile of v1, /device:TPU:32, one launch (start us, length us, event | category | flops | bytes accessed | tf_op | source)
XLA Modules:
  0.0 627.1 jit_solution(23702905049726879)
XLA Ops:
  9.7 1.4 scatter_custom_fusion
  11.8 14.2 %all-to-all-start = ((s32[64,1,8]{2,1,0:T(1,128)}), s32[64,1,8]{2,1,0:T(1,128)S(1)}, u32[]{:S(2)}, u32[]{:S(2)}) async-start(s32[64,1,8]{2,1,0:T(1,128)} %bitcast.6), calls=%async_computation | async-start | bytes 65536 | tf_op jit(solution)/shard_map/all_to_all | solution.py:81
  26.1 3.7 scatter_custom_fusion.1
  29.8 7.1 %all-to-all-done = s32[64,1,8]{2,1,0:T(1,128)S(1)} async-done(((s32[64,1,8]{2,1,0:T(1,128)}), s32[64,1,8]{2,1,0:T(1,128)S(1)}, u32[]{:S(2)}, u32[]{:S(2)}) %all-to-all-start) | async-done | bytes 2080 | tf_op jit(solution)/shard_map/all_to_all | solution.py:81
  36.9 6.3 %all-to-all-start.1 = ((bf16[64,8,1536]{2,1,0:T(8,128)(2,1)}), bf16[64,8,1536]{2,1,0:T(8,128)(2,1)}, u32[]{:S(2)}, u32[]{:S(2)}) async-start(bf16[64,8,1536]{2,1,0:T(8,128)(2,1)} %bitcast.123), calls=%async_computation.1 | async-start | bytes 3145728 | tf_op jit(solution)/shard_map/all_to_all | solution.py:74
  44.5 39.3 %all-to-all-done.1 = bf16[64,8,1536]{2,1,0:T(8,128)(2,1)} async-done(((bf16[64,8,1536]{2,1,0:T(8,128)(2,1)}), bf16[64,8,1536]{2,1,0:T(8,128)(2,1)}, u32[]{:S(2)}, u32[]{:S(2)}) %all-to-all-start.1) | async-done | bytes 1572896 | tf_op jit(solution)/shard_map/all_to_all | solution.py:74
  83.7 4.0 scatter_custom_fusion.2
  88.3 5.1 convolution_convert_fusion
  94.4 1.9 copy.31
  96.3 3.8 stack.2
  100.1 7.3 %all-to-all-start.2 = ((bf16[256,6,1536]{2,1,0:T(8,128)(2,1)}), bf16[256,6,1536]{2,1,0:T(8,128)(2,1)}, u32[]{:S(2)}, u32[]{:S(2)}) async-start(bf16[256,6,1536]{2,1,0:T(8,128)(2,1)} %stack.2), calls=%async_computation.2 | async-start | bytes 12582912 | tf_op jit(solution)/shard_map/all_to_all | solution.py:12
  111.6 26.4 %all-gather.7.cloned.1.call-done = bf16[1024,8,96]{0,2,1:T(8,128)(2,1)} async-done(((bf16[256,8,96]{0,2,1:T(8,128)(2,1)}), bf16[1024,8,96]{0,2,1:T(8,128)(2,1)}) %all-gather.7.cloned.1.call-update) | async-done | bytes 1572880 | tf_op jit(solution)/shard_map/all_gather | solution.py:132
  138.0 2.7 copy.43
  140.8 40.2 %all-gather.5.cloned.1.call-done = bf16[1024,8,96]{0,2,1:T(8,128)(2,1)} async-done(((bf16[256,8,96]{0,2,1:T(8,128)(2,1)}), bf16[1024,8,96]{0,2,1:T(8,128)(2,1)}) %all-gather.5.cloned.1.call-update) | async-done | bytes 1572880 | tf_op jit(solution)/shard_map/all_gather | solution.py:131
  181.0 2.8 copy.44
  183.7 22.2 %while.15 = (s32[]{:T(128)}, f32[8,256]{1,0:T(8,128)S(1)}, f32[8,256]{1,0:T(8,128)S(1)}, f32[8,256,96]{1,2,0:T(8,128)}, s32[256]{0:T(256)S(1)}, /*index=5*/s32[2...) while((s32[]{:T(128)}, f32[8,256]{1,0:T(8,128)S(1)}, ...), condition=%wide.region_11.12_spmd.clone, body=%wide.region_8.11_spmd.clone.sunk | while | flops 417146880 | bytes 33564948 | solution.py:146
  184.0 4.0 fusion.139
  188.0 3.3 fusion.140
  191.4 3.3 fusion.142
  195.0 4.0 fusion.139
  199.0 3.3 fusion.140
  202.4 3.5 fusion.142
  205.9 1.3 divide_convert_fusion
  208.2 1.2 copy-done.4
  209.7 38.7 %all-to-all-done.2 = bf16[256,6,1536]{2,1,0:T(8,128)(2,1)} async-done(((bf16[256,6,1536]{2,1,0:T(8,128)(2,1)}), bf16[256,6,1536]{2,1,0:T(8,128)(2,1)}, u32[]{:S(2)}, u32[]{:S(2)}) %all-to-all-start.2) | async-done | bytes 4718624 | tf_op jit(solution)/shard_map/all_to_all | solution.py:12
  248.4 8.5 %reshape.297 = bf16[1536,1536]{1,0:T(8,128)(2,1)} reshape(bf16[256,6,1536]{2,1,0:T(8,128)(2,1)} %all-to-all-done.2) | data formatting | bytes 9437184 | tf_op jit(solution)/shard_map/reshape | solution.py:12
  256.9 4.3 fusion.31
  261.4 2.0 collective-permute-start
  263.4 1.3 collective-permute-start.1
  265.0 341.0 %all-gather.9.cloned.1.call-done = bf16[256,6,768]{2,1,0:T(8,128)(2,1)} async-done(((bf16[1,6,768]{2,1,0:T(8,128)(2,1)}), bf16[256,6,768]{2,1,0:T(8,128)(2,1)}) %all-gather.9.cloned.1.call-update) | async-done | bytes 2359312 | tf_op jit(solution)/shard_map/all_gather | solution.py:180
  606.0 5.1 reshape.323
  611.3 9.2 %fusion.23 = bf16[1,256,1536]{2,1,0:T(8,128)(2,1)} fusion(f32[256,1536]{1,0:T(8,128)} %copy-done.4, bf16[1536,768]{1,0:T(8,128)(2,1)} %reshape.323, f32[288,768]{1,0:T(8,128)S(1)} %maximum_convert_fusion, f32[768]{0:T(1024)S(1)} %copy-done.28, f32[768]{0:T(1024)S(1)} %copy-done.29, f32[256]{0:T(256)S(1)} %get-tuple-element.185, ...), kind=kOutput, calls=%fused_computation.37 | convolution fusion | flops 624820224 | bytes 30056448 | tf_op jit(solution)/shard_map/dot_general | solution.py:178
  (125 shorter events, 13.3 us)
Async XLA Ops:
  6.5 200.7 %copy-start = (bf16[768,1536]{1,0:T(8,128)(2,1)S(1)}, bf16[768,1536]{1,0:T(8,128)(2,1)}, u32[]{:S(2)}) copy-start(bf16[768,1536]{1,0:T(8,128)(2,1)} %param.21) | copy-start | bytes 7077892
  11.8 25.1 %all-to-all-start = ((s32[64,1,8]{2,1,0:T(1,128)}), s32[64,1,8]{2,1,0:T(1,128)S(1)}, u32[]{:S(2)}, u32[]{:S(2)}) async-start(s32[64,1,8]{2,1,0:T(1,128)} %bitcast.6), calls=%async_computation | async-start | bytes 65536 | tf_op jit(solution)/shard_map/all_to_all | solution.py:81
  36.9 46.8 %all-to-all-start.1 = ((bf16[64,8,1536]{2,1,0:T(8,128)(2,1)}), bf16[64,8,1536]{2,1,0:T(8,128)(2,1)}, u32[]{:S(2)}, u32[]{:S(2)}) async-start(bf16[64,8,1536]{2,1,0:T(8,128)(2,1)} %bitcast.123), calls=%async_computation.1 | async-start | bytes 3145728 | tf_op jit(solution)/shard_map/all_to_all | solution.py:74
  43.2 94.8 %all-gather.7.cloned.1.call-start = ((), (), s32[]{:S(2)}) async-start(), calls=%async_computation.4 | async-start | bytes 1966080 | tf_op jit(solution)/shard_map/all_gather | solution.py:132
  100.1 9.1 %copy-start.7 = (s32[1,1024]{1,0:T(1,128)S(1)}, s32[1,1024]{1,0:T(1,128)}, u32[]{:S(2)}) copy-start(s32[1,1024]{1,0:T(1,128)} %param.17) | copy-start | bytes 12292
  100.1 9.7 %copy-start.8 = (s32[1,2,8]{2,1,0:T(2,128)S(1)}, s32[1,2,8]{2,1,0:T(2,128)}, u32[]{:S(2)}) copy-start(s32[1,2,8]{2,1,0:T(2,128)} %param.18) | copy-start | bytes 196
  100.1 9.8 %copy-start.6 = (f32[32,768]{1,0:T(8,128)S(1)}, f32[32,768]{1,0:T(8,128)}, u32[]{:S(2)}) copy-start(f32[32,768]{1,0:T(8,128)} %param.25) | copy-start | bytes 294916
  100.1 148.3 %all-to-all-start.2 = ((bf16[256,6,1536]{2,1,0:T(8,128)(2,1)}), bf16[256,6,1536]{2,1,0:T(8,128)(2,1)}, u32[]{:S(2)}, u32[]{:S(2)}) async-start(bf16[256,6,1536]{2,1,0:T(8,128)(2,1)} %stack.2), calls=%async_computation.2 | async-start | bytes 12582912 | tf_op jit(solution)/shard_map/all_to_all | solution.py:12
  107.4 73.5 %all-gather.5.cloned.1.call-start = ((), (), s32[]{:S(2)}) async-start(), calls=%async_computation.3 | async-start | bytes 1966080 | tf_op jit(solution)/shard_map/all_gather | solution.py:131
  108.4 497.5 %all-gather.9.cloned.1.call-start = ((), (), s32[]{:S(2)}) async-start(), calls=%async_computation.5 | async-start | bytes 3158016 | tf_op jit(solution)/shard_map/all_gather | solution.py:180
  209.7 47.2 %copy-start.27 = (f32[1536]{0:T(1024)S(1)}, f32[1536]{0:T(1024)}, u32[]{:S(2)}) copy-start(f32[1536]{0:T(1024)} %param.22) | copy-start | bytes 18436
  261.4 349.7 %collective-permute-start = (bf16[16,768]{1,0:T(8,128)(2,1)S(1)}, bf16[16,768]{1,0:T(8,128)(2,1)S(1)}, u32[]{:S(2)}, u32[]{:S(2)}) collective-permute-start(bf16[16,768]{1,0:T(8,128)(2,1)S(1)} %get-tuple-element.182), channel_id=1, source_target_pairs={{0,1},{1,2},{2,3},{4,5},{5,6},{6,7},{8,9},{9,10},{10,11},{12,13},{... | collective-permute-start | bytes 73736 | tf_op jit(solution)/shard_map/ppermute | solution.py:23
  263.4 347.7 %collective-permute-start.1 = (bf16[16,768]{1,0:T(8,128)(2,1)S(1)}, bf16[16,768]{1,0:T(8,128)(2,1)S(1)}, u32[]{:S(2)}, u32[]{:S(2)}) collective-permute-start(bf16[16,768]{1,0:T(8,128)(2,1)S(1)} %get-tuple-element.183), channel_id=1, source_target_pairs={{1,0},{2,1},{3,2},{5,4},{6,5},{7,6},{9,8},{10,9},{11,10},{13,12},{... | collective-permute-start | bytes 73736 | tf_op jit(solution)/shard_map/ppermute | solution.py:25
  264.8 346.4 %copy-start.9 = (f32[256]{0:T(256)S(1)}, f32[256]{0:T(256)}, u32[]{:S(2)}) copy-start(f32[256]{0:T(256)} %get-tuple-element.199) | copy-start | bytes 3076
  264.8 346.4 %copy-start.10 = (f32[256]{0:T(256)S(1)}, f32[256]{0:T(256)}, u32[]{:S(2)}) copy-start(f32[256]{0:T(256)} %get-tuple-element.200) | copy-start | bytes 3076
  264.8 346.4 %copy-start.11 = (f32[256]{0:T(256)S(1)}, f32[256]{0:T(256)}, u32[]{:S(2)}) copy-start(f32[256]{0:T(256)} %get-tuple-element.201) | copy-start | bytes 3076
  264.8 346.4 %copy-start.12 = (f32[256]{0:T(256)S(1)}, f32[256]{0:T(256)}, u32[]{:S(2)}) copy-start(f32[256]{0:T(256)} %get-tuple-element.202) | copy-start | bytes 3076
  264.8 346.4 %copy-start.13 = (f32[256]{0:T(256)S(1)}, f32[256]{0:T(256)}, u32[]{:S(2)}) copy-start(f32[256]{0:T(256)} %get-tuple-element.203) | copy-start | bytes 3076
  264.8 346.4 %copy-start.14 = (f32[256]{0:T(256)S(1)}, f32[256]{0:T(256)}, u32[]{:S(2)}) copy-start(f32[256]{0:T(256)} %get-tuple-element.204) | copy-start | bytes 3076
  264.9 346.4 %copy-start.15 = (f32[256]{0:T(256)S(1)}, f32[256]{0:T(256)}, u32[]{:S(2)}) copy-start(f32[256]{0:T(256)} %get-tuple-element.205) | copy-start | bytes 3076
  264.9 346.4 %copy-start.16 = (f32[256]{0:T(256)S(1)}, f32[256]{0:T(256)}, u32[]{:S(2)}) copy-start(f32[256]{0:T(256)} %get-tuple-element.206) | copy-start | bytes 3076
  264.9 346.4 %copy-start.17 = (f32[256]{0:T(256)S(1)}, f32[256]{0:T(256)}, u32[]{:S(2)}) copy-start(f32[256]{0:T(256)} %get-tuple-element.207) | copy-start | bytes 3076
  264.9 346.4 %copy-start.18 = (f32[256]{0:T(256)S(1)}, f32[256]{0:T(256)}, u32[]{:S(2)}) copy-start(f32[256]{0:T(256)} %get-tuple-element.208) | copy-start | bytes 3076
  264.9 346.4 %copy-start.19 = (f32[256]{0:T(256)S(1)}, f32[256]{0:T(256)}, u32[]{:S(2)}) copy-start(f32[256]{0:T(256)} %get-tuple-element.209) | copy-start | bytes 3076
  264.9 346.4 %copy-start.20 = (f32[256]{0:T(256)S(1)}, f32[256]{0:T(256)}, u32[]{:S(2)}) copy-start(f32[256]{0:T(256)} %get-tuple-element.210) | copy-start | bytes 3076
  264.9 346.4 %copy-start.21 = (f32[256]{0:T(256)S(1)}, f32[256]{0:T(256)}, u32[]{:S(2)}) copy-start(f32[256]{0:T(256)} %get-tuple-element.211) | copy-start | bytes 3076
  264.9 346.4 %copy-start.22 = (f32[256]{0:T(256)S(1)}, f32[256]{0:T(256)}, u32[]{:S(2)}) copy-start(f32[256]{0:T(256)} %get-tuple-element.212) | copy-start | bytes 3076
  264.9 346.4 %copy-start.23 = (f32[256]{0:T(256)S(1)}, f32[256]{0:T(256)}, u32[]{:S(2)}) copy-start(f32[256]{0:T(256)} %get-tuple-element.213) | copy-start | bytes 3076
  264.9 346.4 %copy-start.24 = (f32[256]{0:T(256)S(1)}, f32[256]{0:T(256)}, u32[]{:S(2)}) copy-start(f32[256]{0:T(256)} %get-tuple-element.214) | copy-start | bytes 3076
  265.0 346.4 %copy-start.25 = (f32[256]{0:T(256)S(1)}, f32[256]{0:T(256)}, u32[]{:S(2)}) copy-start(f32[256]{0:T(256)} %get-tuple-element.215) | copy-start | bytes 3076
  265.0 346.4 %copy-start.28 = (f32[768]{0:T(1024)S(1)}, f32[768]{0:T(1024)}, u32[]{:S(2)}) copy-start(f32[768]{0:T(1024)} %param.27) | copy-start | bytes 9220
  265.0 346.4 %copy-start.29 = (f32[768]{0:T(1024)S(1)}, f32[768]{0:T(1024)}, u32[]{:S(2)}) copy-start(f32[768]{0:T(1024)} %param.26) | copy-start | bytes 9220
  (7 other events, 27.0 us)
Sparse Core Ops, SparseCore 0:
  96.5 41.5 all-gather.6
  139.8 41.0 all-gather.4
  182.9 423.0 all-gather.8
